TPU v7x, 32 devices: a whole 2x2x4 slice. The times are simulated.
32 devices in a mesh: grp: 4 (over y, x), seq: 4 (over z), mlp: 2 (over core).
Axes of the slice: x: 2, y: 2, z: 4, core: 2. Of those that a mesh axis runs over, the one named last changes fastest.
Arguments:
- queries: bfloat16 [16, 4, 4096], P('grp'), may hold values from -6 to 6
- new_keys: bfloat16 [16, 4, 4096], P(('grp', 'seq')), may hold values from -6 to 6
- new_values: bfloat16 [16, 4, 4096], P(('grp', 'seq')), may hold values from -6 to 6
- prefix_keys: bfloat16 [4, 2048, 4096], P('grp', ('seq', 'mlp')), may hold values from -250 to 250
- prefix_values: bfloat16 [4, 2048, 4096], P('grp', ('seq', 'mlp')), may hold values from -6 to 6
- tail_keys: bfloat16 [16, 256, 4096], P(('grp', 'seq'), 'mlp'), may hold values from -6 to 6
- tail_values: bfloat16 [16, 256, 4096], P(('grp', 'seq'), 'mlp'), may hold values from -6 to 6
- prefix_len: int32 [4], P('grp'), may hold values from 1 to 2048, as said below
- tail_len: int32 [16], P('grp'), may hold values from 0 to 256, as said below
- resid: bfloat16 [16, 4, 4096], P('grp', None, ('seq', 'mlp')), may hold values from -12 to 12
- w_out: bfloat16 [4096, 4096], P(None, ('seq', 'mlp')), may hold values from -0.09375 to 0.09375
- ln_gain: bfloat16 [4096], P(('seq', 'mlp')), may hold values from 0.25 to 1.75
- w_up: bfloat16 [4096, 16384], P(('seq', 'mlp'), 'grp'), may hold values from -0.09375 to 0.09375
- w_down: bfloat16 [16384, 4096], P('grp', ('seq', 'mlp')), may hold values from -0.046875 to 0.046875
Outputs:
- out: float32 [16, 4, 4096], P('grp', None, ('seq', 'mlp'))
Inputs may be any that keep to these rules, and one draw needn't show every extreme that they name: `prefix_len`: every group's live prefix is 1 to 2048 slots; in every draw some group's prefix fills all 2048 slots. `tail_len`: A request's live tail is 0 to 256 slots; in every draw some request's tail fills all 256 slots.
All inputs are finite; a program needn't handle non-finite values.
Results may differ from a plain program's by a relative error of at most 0.0075.
Values may be sent and summed in bfloat16 or wider, within the bound.
A program may use at most 128 MiB of HBM per device.

v0:
```python
import math
import jax
import jax.numpy as jnp
from jax import lax
from jax.sharding import PartitionSpec as P

D = 4096
H = 32
NEG = -1e30


def merged(value, axis, join):
    pieces = jax.tree.map(lambda part: lax.all_gather(part, axis), value)
    head = jax.tree.map(lambda part: part[0], pieces)
    tail = jax.tree.map(lambda part: part[1:], pieces)
    so_far, _ = lax.scan(lambda so_far, piece: (join(so_far, piece), None), head, tail)
    return so_far


def head_slopes(count):
    return jnp.power(2.0, -8.0 * (jnp.arange(count, dtype=jnp.float32) + 1.0) / count)


def attend(query_rows, key_block, value_block, query_pos, key_pos, key_mask):
    head_count = query_rows.shape[1]
    inv_scale = 1.0 / math.sqrt(query_rows.shape[2])
    scores = (
        jnp.einsum("qhd,khd->hqk", query_rows, key_block, preferred_element_type=jnp.float32)
        * inv_scale
    )
    distance = (query_pos[:, None] - key_pos[None, :]).astype(jnp.float32)
    scores = scores - head_slopes(head_count)[:, None, None] * distance[None, :, :]
    scores = jnp.where(key_mask, scores, NEG)
    row_max = jnp.max(scores, axis=2)
    weights = jnp.where(key_mask, jnp.exp(scores - row_max[:, :, None]), 0.0)
    weight_sum = jnp.sum(weights, axis=2)
    mixed_sum = jnp.einsum(
        "hqk,khd->qhd",
        weights.astype(jnp.bfloat16),
        value_block,
        preferred_element_type=jnp.float32,
    )
    return (row_max.T, weight_sum.T, mixed_sum)


def join_parts(first, second):
    best_max = jnp.maximum(first[0], second[0])
    factor_one = jnp.exp(first[0] - best_max)
    factor_two = jnp.exp(second[0] - best_max)
    return (
        best_max,
        first[1] * factor_one + second[1] * factor_two,
        first[2] * factor_one[:, :, None] + second[2] * factor_two[:, :, None],
    )


def body(
    queries,
    new_keys,
    new_values,
    prefix_keys,
    prefix_values,
    tail_keys,
    tail_values,
    prefix_len,
    tail_len,
    resid,
    w_out,
    ln_gain,
    w_up,
    w_down,
):
    group_req, step_count, model_width = queries.shape
    head_dim = model_width // H
    row_count = group_req * step_count
    seq_index = lax.axis_index("seq")
    core_index = lax.axis_index("mlp")
    block_len = prefix_keys.shape[1]
    tail_block = tail_keys.shape[1]
    block_start = (seq_index * lax.axis_size("mlp") + core_index) * block_len
    prefix_end = prefix_len[0]
    step_index = jnp.arange(step_count, dtype=jnp.int32)
    query_pos = prefix_end + jnp.repeat(tail_len, step_count) + jnp.tile(step_index, group_req)
    query_rows = queries.reshape(row_count, H, head_dim)
    key_pos = block_start + jnp.arange(block_len, dtype=jnp.int32)
    key_live = key_pos < prefix_end
    own_len = lax.dynamic_index_in_dim(tail_len, seq_index, 0, keepdims=False)
    own_rows = lax.dynamic_slice_in_dim(query_rows, seq_index * step_count, step_count, 0)
    own_pos = prefix_end + own_len + step_index
    tail_index = core_index * tail_block + jnp.arange(tail_block, dtype=jnp.int32)
    partial_value = attend(
        query_rows,
        prefix_keys[0].reshape(block_len, H, head_dim),
        prefix_values[0].reshape(block_len, H, head_dim),
        query_pos,
        key_pos,
        key_live[None, None, :],
    )
    tail_result = attend(
        own_rows,
        tail_keys[0].reshape(tail_block, H, head_dim),
        tail_values[0].reshape(tail_block, H, head_dim),
        own_pos,
        prefix_end + tail_index,
        (tail_index < own_len)[None, None, :],
    )
    self_mask = (step_index[None, :] <= step_index[:, None]) & (core_index == 0)
    self_result = attend(
        own_rows,
        new_keys[0].reshape(step_count, H, head_dim),
        new_values[0].reshape(step_count, H, head_dim),
        own_pos,
        own_pos,
        self_mask[None, :, :],
    )
    own_slice = tuple(
        (
            lax.dynamic_slice_in_dim(member, seq_index * step_count, step_count, 0)
            for member in partial_value
        )
    )
    own_part = join_parts(join_parts(own_slice, tail_result), self_result)
    partial_value = tuple(
        (
            lax.dynamic_update_slice_in_dim(member, update, seq_index * step_count, 0)
            for member, update in zip(partial_value, own_part)
        )
    )
    row_max, weight_sum, mixed_sum = merged(
        (partial_value[0], partial_value[1], partial_value[2]), ("seq", "mlp"), join_parts
    )
    attention = (
        (mixed_sum / weight_sum[:, :, None]).astype(jnp.bfloat16).reshape(row_count, model_width)
    )
    width_block = resid.shape[2]
    stream = resid.astype(jnp.float32).reshape(row_count, width_block) + jnp.dot(
        attention, w_out, preferred_element_type=jnp.float32
    )
    row_sums, squares = lax.psum(
        (jnp.sum(stream, axis=1), jnp.sum(stream * stream, axis=1)), ("seq", "mlp")
    )
    row_mean = row_sums / D
    row_var = squares / D - row_mean * row_mean
    hidden = (
        (stream - row_mean[:, None])
        * lax.rsqrt(row_var[:, None] + 1e-05)
        * ln_gain.astype(jnp.float32)
    ).astype(jnp.bfloat16)
    lifted = jnp.dot(
        lax.all_gather(hidden, "grp", axis=0, tiled=True), w_up, preferred_element_type=jnp.float32
    )
    summed = lax.psum(lifted, ("seq", "mlp"))
    activated = jax.nn.gelu(summed, approximate=False).astype(jnp.bfloat16)
    projected = lax.psum_scatter(
        jnp.dot(activated, w_down, preferred_element_type=jnp.float32),
        "grp",
        scatter_dimension=0,
        tiled=True,
    )
    return (stream + projected).reshape(group_req, step_count, width_block)


def solution(mesh):
    return jax.shard_map(
        body,
        mesh=mesh,
        in_specs=(
            P("grp", None, None),
            P(("grp", "seq"), None, None),
            P(("grp", "seq"), None, None),
            P("grp", ("seq", "mlp"), None),
            P("grp", ("seq", "mlp"), None),
            P(("grp", "seq"), "mlp", None),
            P(("grp", "seq"), "mlp", None),
            P("grp"),
            P("grp"),
            P("grp", None, ("seq", "mlp")),
            P(None, ("seq", "mlp")),
            P(("seq", "mlp")),
            P(("seq", "mlp"), "grp"),
            P("grp", ("seq", "mlp")),
        ),
        out_specs=P("grp", None, ("seq", "mlp")),
        check_vma=False,
    )
```

profile of v0, /device:TPU:0, one launch (start us, length us, event | category | flops | bytes accessed | tf_op | source)
XLA Modules:
  0.0 181.5 jit_solution(5606925134826433128)
XLA Ops:
  7.4 1.2 dynamic_slice.28
  9.2 0.6 fusion.102
  9.9 1.1 reshape.182
  11.0 1.4 copy.98
  12.5 0.7 fusion.143
  13.8 0.5 copy.97
  14.4 1.2 fusion.142
  16.9 0.5 copy.99
  17.4 1.0 fusion.3
  19.1 0.5 fusion.22
  19.8 0.8 copy.92
  21.0 15.8 %all_gather.32 = f32[8,16,32]{2,1,0:T(8,128)S(1)} all-gather(f32[1,16,32]{2,1,0:T(8,128)S(1)} %copy.83), channel_id=1, replica_groups=mesh['grp'=4,'seq'=4,'mlp'=2] {'seq','mlp'}, dimensions={0}, use_global_device_ids=true | all-gather | bytes 18432 | tf_op jit(solution)/shard_map/all_gather | solution.py:13
  37.2 14.1 %all_gather.29 = f32[8,16,32]{2,1,0:T(8,128)S(1)} all-gather(f32[1,16,32]{2,1,0:T(8,128)S(1)} %copy.76), channel_id=1, replica_groups=mesh['grp'=4,'seq'=4,'mlp'=2] {'seq','mlp'}, dimensions={0}, use_global_device_ids=true | all-gather | bytes 18432 | tf_op jit(solution)/shard_map/all_gather | solution.py:13
  51.4 1.7 all-gather.2.cloned.1.call-done
  53.1 1.7 slice.29
  54.8 1.0 slice_bitcast_fusion
  55.8 2.2 %while.14 = (s32[]{:T(128)}, f32[16,32]{1,0:T(8,128)S(1)}, f32[16,32]{1,0:T(8,128)S(1)}, f32[16,32,128]{2,1,0:T(8,128)S(1)}, f32[7,16,32]{2,1,0:T(8,128)S(1)}, /...) while((s32[]{:T(128)}, f32[16,32]{1,0:T(8,128)S(1)}, f32[16,32]{1,0:T(8,128)S(1)}, ...), condition=%wide.region_7.8_spmd, body=%wide.region_6.7_spmd.sunk | while | flops 199682 | bytes 807005 | solution.py:16
  55.8 0.3 fusion.153
  56.1 0.3 fusion.153
  56.4 0.3 fusion.153
  56.8 0.3 fusion.153
  57.1 0.3 fusion.153
  57.4 0.3 fusion.153
  58.1 3.0 %fusion.137 = (f32[16]{0:T(128)S(1)}, f32[16]{0:T(128)S(1)}, f32[16,512]{1,0:T(8,128)S(1)}) fusion(f32[16,512]{1,0:T(8,128)S(1)} %reshape.186, bf16[4096,512]{1,0:T(8,128)(2,1)} %param.26, bf16[2,8,32,128]{3,2,1,0:T(8,128)(2,1)S(1)} %bitcast.177), kind=kOutput, calls=%fused_computation.181 | convolution fusion | flops 67141600 | bytes 4391040 | tf_op jit(solution)/shard_map/dot_general | solution.py:136
  61.1 15.5 %all-reduce = (f32[16]{0:T(128)S(1)}, f32[16]{0:T(128)S(1)}) all-reduce(f32[16]{0:T(128)S(1)} %get-tuple-element.60, f32[16]{0:T(128)S(1)} %get-tuple-element.59), channel_id=1, replica_groups=mesh['grp'=4,'seq'=4,'mlp'=2] {'seq','mlp'}, use_global_device_ids=true, to_apply=%region_11.12 | all-reduce | flops 32 | bytes 256 | tf_op jit(solution)/shard_map/psum | solution.py:139
  76.6 8.1 %all_gather.36 = bf16[64,512]{1,0:T(8,128)(2,1)S(1)} all-gather(bf16[16,512]{1,0:T(8,128)(2,1)S(1)} %multiply_convert_fusion), channel_id=1, replica_groups=mesh['grp'=4,'seq'=4,'mlp'=2] {'grp'}, dimensions={0}, use_global_device_ids=true | all-gather | bytes 81920 | tf_op jit(solution)/shard_map/all_gather | solution.py:150
  84.8 4.1 %fusion.144 = f32[64,4096]{1,0:T(8,128)} fusion(bf16[64,512]{1,0:T(8,128)(2,1)S(1)} %all_gather.36, bf16[512,4096]{1,0:T(8,128)(2,1)} %param.28), kind=kOutput, calls=%fused_computation.184 | convolution fusion | flops 268435456 | bytes 5308416 | tf_op jit(solution)/shard_map/dot_general | solution.py:149
  88.9 56.1 %all-reduce.3.cloned.1.call-done = f32[64,4096]{1,0:T(8,128)} async-done(((f32[64,4096]{1,0:T(8,128)}), f32[64,4096]{1,0:T(8,128)}) %all-reduce.3.cloned.1.call-update) | async-done | bytes 1048592 | tf_op jit(solution)/shard_map/psum | solution.py:152
  145.1 5.5 %fusion.37 = f32[64,512]{1,0:T(8,128)} fusion(bf16[4096,512]{1,0:T(8,128)(2,1)} %param.29, f32[64,4096]{1,0:T(8,128)} %all-reduce.3.cloned.1.call-done), kind=kOutput, calls=%fused_computation.49 | convolution fusion | flops 285474816 | bytes 5373952 | tf_op jit(solution)/shard_map/dot_general | solution.py:155
  150.6 22.9 %reduce-scatter.2.cloned.1.call-done = f32[16,512]{1,0:T(8,128)} async-done(((f32[64,512]{1,0:T(8,128)}), f32[16,512]{1,0:T(8,128)}) %reduce-scatter.2.cloned.1.call-update) | async-done | bytes 32784 | tf_op jit(solution)/shard_map/reduce_scatter | solution.py:154
  173.6 0.8 add.168
  174.3 0.6 reshape.184
  (77 shorter events, 4.4 us)
Async XLA Ops:
  6.5 13.1 %copy-start = (bf16[1,4,4096]{2,1,0:T(4,128)(2,1)S(1)}, bf16[1,4,4096]{2,1,0:T(4,128)(2,1)}, u32[]{:S(2)}) copy-start(bf16[1,4,4096]{2,1,0:T(4,128)(2,1)} %param.18) | copy-start | bytes 98308
  6.5 7.1 %copy-start.7 = (s32[4]{0:T(128)S(1)}, s32[4]{0:T(128)}, u32[]{:S(2)}) copy-start(s32[4]{0:T(128)} %param.24) | copy-start | bytes 52
  6.5 7.2 %copy-start.1 = (bf16[1,256,4096]{2,1,0:T(8,128)(2,1)S(1)}, bf16[1,256,4096]{2,1,0:T(8,128)(2,1)}, u32[]{:S(2)}) copy-start(bf16[1,256,4096]{2,1,0:T(8,128)(2,1)} %param.19) | copy-start | bytes 6291460
  6.5 46.6 %all-gather.2.cloned.1.call-start = ((), (), s32[]{:S(2)}) async-start(), calls=%async_computation.1 | async-start | bytes 2359296 | tf_op jit(solution)/shard_map/all_gather | solution.py:13
  14.3 1.8 copy-start.4
  14.3 2.6 %copy-start.2 = (bf16[1,256,4096]{2,1,0:T(8,128)(2,1)S(1)}, bf16[1,256,4096]{2,1,0:T(8,128)(2,1)}, u32[]{:S(2)}) copy-start(bf16[1,256,4096]{2,1,0:T(8,128)(2,1)} %param.20) | copy-start | bytes 6291460
  17.3 1.2 copy-start.3
  18.8 32.5 %copy-start.5 = (bf16[4,4,512]{2,1,0:T(4,128)(2,1)S(1)}, bf16[4,4,512]{2,1,0:T(4,128)(2,1)}, u32[]{:S(2)}) copy-start(bf16[4,4,512]{2,1,0:T(4,128)(2,1)} %param.25) | copy-start | bytes 49156
  18.8 32.5 %copy-start.6 = (bf16[512]{0:T(512)(128)(2,1)S(1)}, bf16[512]{0:T(512)(128)(2,1)}, u32[]{:S(2)}) copy-start(bf16[512]{0:T(512)(128)(2,1)} %param.27) | copy-start | bytes 3076
  20.6 124.4 %all-reduce.3.cloned.1.call-start = ((), (), s32[]{:S(2)}) async-start(), calls=%async_computation.2 | async-start | bytes 2097152 | tf_op jit(solution)/shard_map/psum | solution.py:152
  88.9 84.7 %reduce-scatter.2.cloned.1.call-start = ((), (), s32[]{:S(2)}) async-start(), calls=%async_computation.3 | async-start | bytes 163840 | tf_op jit(solution)/shard_map/reduce_scatter | solution.py:154
Sparse Core Ops, SparseCore 0:
  20.8 32.3 all-gather.1
  89.0 56.0 all-reduce.2
  150.7 22.7 reduce-scatter.1
where the time goes:
time: 182 us; the launch traced here: 181 us
  waiting for transfers between devices  80.9 us (44%)
  blocking collectives  53.5 us (29%)
  matrix products  16.5 us (9%)
  between operations  14.8 us (8%)
  local copies, waits for them, and re-layouts  11 us (6%)
  other arithmetic  4.55 us (2%)
    psum x1, waiting for transfers between devices, body(): summed = lax.psum(lifted, ('seq', 'mlp'))  56.1 us
    all_gather x2, blocking collectives, merged(): pieces = jax.tree.map(lambda part: lax.all_gather(part, axis), value)  29.9 us
    reduce_scatter x1, waiting for transfers between devices, body(): lax.psum_scatter(jnp.dot(activated, w_down, preferred_element_type=jnp.fl...  22.9 us
    psum x1, blocking collectives, body(): lax.psum((jnp.sum(stream, axis=1), jnp.sum(stream * stream, axis=1)), ('s...  15.5 us
    all_gather x1, blocking collectives, body(): lax.all_gather(hidden, 'grp', axis=0, tiled=True)  8.13 us
    dot_general x1, matrix products, body(): jnp.dot(activated, w_down, preferred_element_type=jnp.float32)  5.52 us
    dot_general x1, matrix products, body(): jnp.dot(lax.all_gather(hidden, 'grp', axis=0, tiled=True), w_up, preferre...  4.1 us
  transfers between devices with their start and end apart: 3, of which 3 were waited for; matrix products, arithmetic and copies ran while one was open for 0% of the time, Pallas kernels for 0%

commit v1 on v0

--- a/solution.py
+++ b/solution.py
@@ -149,7 +149,7 @@
     lifted = jnp.dot(
         lax.all_gather(hidden, "grp", axis=0, tiled=True), w_up, preferred_element_type=jnp.float32
     )
-    summed = lax.psum(lifted, ("seq", "mlp"))
+    summed = jnp.sum(lax.all_gather(lifted, ("seq", "mlp")), axis=0)
     activated = jax.nn.gelu(summed, approximate=False).astype(jnp.bfloat16)
     projected = lax.psum_scatter(
         jnp.dot(activated, w_down, preferred_element_type=jnp.float32),

time: 182 us -> 215 us (1.18)
  waiting for transfers between devices: 80.9 us -> 104 us
  other arithmetic: 4.55 us -> 12.7 us
    all_gather x0 -> x1, waiting for transfers between devices: none -> 79.4 us  [body(): summed = jnp.sum(lax.all_gather(lifted, ('seq', 'mlp')), axis=0)]
    psum x1 -> x0, waiting for transfers between devices: 56.1 us -> none  [body(): summed = lax.psum(lifted, ('seq', 'mlp'))]
    reduce_sum x0 -> x1, other arithmetic: none -> 3.97 us  [body(): summed = jnp.sum(lax.all_gather(lifted, ('seq', 'mlp')), axis=0)]
where the time goes in v1:
time: 215 us; the launch traced here: 214 us
  waiting for transfers between devices  104 us (48%)
  blocking collectives  53.6 us (25%)
  matrix products  17.2 us (8%)
  between operations  14.8 us (7%)
  other arithmetic  12.7 us (6%)
  local copies, waits for them, and re-layouts  11.8 us (5%)
    all_gather x1, waiting for transfers between devices, body(): summed = jnp.sum(lax.all_gather(lifted, ('seq', 'mlp')), axis=0)  79.4 us
    all_gather x2, blocking collectives, merged(): pieces = jax.tree.map(lambda part: lax.all_gather(part, axis), value)  30.1 us
    reduce_scatter x1, waiting for transfers between devices, body(): lax.psum_scatter(jnp.dot(activated, w_down, preferred_element_type=jnp.fl...  22.5 us
    psum x1, blocking collectives, body(): lax.psum((jnp.sum(stream, axis=1), jnp.sum(stream * stream, axis=1)), ('s...  15.4 us
    all_gather x1, blocking collectives, body(): lax.all_gather(hidden, 'grp', axis=0, tiled=True)  8.13 us
    dot_general x1, matrix products, body(): jnp.dot(activated, w_down, preferred_element_type=jnp.float32)  4.77 us
  transfers between devices with their start and end apart: 3, of which 3 were waited for; matrix products, arithmetic and copies ran while one was open for 0% of the time, Pallas kernels for 0%

profile of v1, /device:TPU:0, one launch (start us, length us, event | category | flops | bytes accessed | tf_op | source)
XLA Modules:
  0.0 214.0 jit_solution(2038052570618687835)
XLA Ops:
  7.2 1.3 dynamic_slice.28
  9.3 1.2 fusion.102
  10.5 0.6 iota_add_fusion.1
  11.1 0.5 broadcast_compare_fusion
  11.6 0.7 broadcast_add_fusion
  12.3 0.6 add.150
  13.0 0.7 subtract_convert_fusion.2
  13.7 1.1 reshape.182
  14.9 0.9 fusion.81
  16.0 0.7 fusion.88
  16.9 1.4 copy.98
  18.3 1.5 fusion.143
  19.9 0.8 fusion.78
  20.8 1.2 copy.100
  22.8 1.2 fusion.142
  25.4 1.0 fusion.3
  27.3 0.8 copy.92
  28.7 15.8 %all_gather.38 = f32[8,16,32]{2,1,0:T(8,128)S(1)} all-gather(f32[1,16,32]{2,1,0:T(8,128)S(1)} %copy.83), channel_id=1, replica_groups=mesh['grp'=4,'seq'=4,'mlp'=2] {'seq','mlp'}, dimensions={0}, use_global_device_ids=true | all-gather | bytes 18432 | tf_op jit(solution)/shard_map/all_gather | solution.py:13
  44.8 14.2 %all_gather.35 = f32[8,16,32]{2,1,0:T(8,128)S(1)} all-gather(f32[1,16,32]{2,1,0:T(8,128)S(1)} %copy.76), channel_id=1, replica_groups=mesh['grp'=4,'seq'=4,'mlp'=2] {'seq','mlp'}, dimensions={0}, use_global_device_ids=true | all-gather | bytes 18432 | tf_op jit(solution)/shard_map/all_gather | solution.py:13
  59.0 1.7 all-gather.4.cloned.1.call-done
  60.7 1.1 slice_bitcast_fusion
  62.3 2.1 while.14
  64.6 3.0 %fusion.137 = (f32[16]{0:T(128)S(1)}, f32[16]{0:T(128)S(1)}, f32[16,512]{1,0:T(8,128)S(1)}) fusion(f32[16,512]{1,0:T(8,128)S(1)} %reshape.186, bf16[4096,512]{1,0:T(8,128)(2,1)} %param.26, bf16[2,8,32,128]{3,2,1,0:T(8,128)(2,1)S(1)} %bitcast.179), kind=kOutput, calls=%fused_computation.181 | convolution fusion | flops 67141600 | bytes 4391040 | tf_op jit(solution)/shard_map/dot_general | solution.py:136
  67.5 15.4 %all-reduce = (f32[16]{0:T(128)S(1)}, f32[16]{0:T(128)S(1)}) all-reduce(f32[16]{0:T(128)S(1)} %get-tuple-element.60, f32[16]{0:T(128)S(1)} %get-tuple-element.59), channel_id=1, replica_groups=mesh['grp'=4,'seq'=4,'mlp'=2] {'seq','mlp'}, use_global_device_ids=true, to_apply=%region_11.12 | all-reduce | flops 32 | bytes 256 | tf_op jit(solution)/shard_map/psum | solution.py:139
  83.0 8.1 %all_gather.42 = bf16[64,512]{1,0:T(8,128)(2,1)S(1)} all-gather(bf16[16,512]{1,0:T(8,128)(2,1)S(1)} %multiply_convert_fusion), channel_id=1, replica_groups=mesh['grp'=4,'seq'=4,'mlp'=2] {'grp'}, dimensions={0}, use_global_device_ids=true | all-gather | bytes 81920 | tf_op jit(solution)/shard_map/all_gather | solution.py:150
  91.1 4.1 %fusion.144 = f32[64,4096]{1,0:T(8,128)} fusion(bf16[64,512]{1,0:T(8,128)(2,1)S(1)} %all_gather.42, bf16[512,4096]{1,0:T(8,128)(2,1)} %param.28), kind=kOutput, calls=%fused_computation.184 | convolution fusion | flops 268435456 | bytes 5308416 | tf_op jit(solution)/shard_map/dot_general | solution.py:149
  95.3 79.4 %all-gather.6.cloned.1.call-done = f32[512,4096]{1,0:T(8,128)} async-done(((f32[64,4096]{1,0:T(8,128)}), f32[512,4096]{1,0:T(8,128)}) %all-gather.6.cloned.1.call-update) | async-done | bytes 8388624 | tf_op jit(solution)/shard_map/all_gather | solution.py:152
  174.7 4.0 %reduce_sum.59 = f32[64,4096]{1,0:T(8,128)S(1)} reduce(f32[8,64,4096]{2,1,0:T(8,128)} %bitcast.169, f32[]{:T(128)} %constant.25.clone.1), dimensions={0}, to_apply=%region_12.13 | reduce | flops 1835008 | bytes 9437188 | tf_op jit(solution)/shard_map/reduce_sum | solution.py:152
  178.7 4.8 %fusion.37 = f32[64,512]{1,0:T(8,128)} fusion(bf16[4096,512]{1,0:T(8,128)(2,1)} %param.29, f32[64,4096]{1,0:T(8,128)S(1)} %reduce_sum.59), kind=kOutput, calls=%fused_computation.49 | convolution fusion | flops 285474816 | bytes 5373952 | tf_op jit(solution)/shard_map/dot_general | solution.py:155
  183.5 22.5 %reduce-scatter.2.cloned.1.call-done = f32[16,512]{1,0:T(8,128)} async-done(((f32[64,512]{1,0:T(8,128)}), f32[16,512]{1,0:T(8,128)}) %reduce-scatter.2.cloned.1.call-update) | async-done | bytes 32784 | tf_op jit(solution)/shard_map/reduce_scatter | solution.py:154
  206.0 0.8 add.166
  206.8 0.6 reshape.184
  (99 shorter events, 7.2 us)
Async XLA Ops:
  6.5 20.6 %copy-start = (bf16[1,4,4096]{2,1,0:T(4,128)(2,1)S(1)}, bf16[1,4,4096]{2,1,0:T(4,128)(2,1)}, u32[]{:S(2)}) copy-start(bf16[1,4,4096]{2,1,0:T(4,128)(2,1)} %param.18) | copy-start | bytes 98308
  6.5 54.2 %all-gather.4.cloned.1.call-start = ((), (), s32[]{:S(2)}) async-start(), calls=%async_computation.1 | async-start | bytes 2359296 | tf_op jit(solution)/shard_map/all_gather | solution.py:13
  6.5 10.3 %copy-start.12 = (f32[32]{0:T(128)}, f32[32]{0:T(128)S(1)}, u32[]{:S(2)}) copy-start(f32[32]{0:T(128)S(1)} %multiply_power_fusion) | copy-start | bytes 388
  13.7 7.2 %copy-start.3 = (bf16[1,128,4096]{2,1,0:T(8,128)(2,1)S(1)}, bf16[1,128,4096]{2,1,0:T(8,128)(2,1)}, u32[]{:S(2)}) copy-start(bf16[1,128,4096]{2,1,0:T(8,128)(2,1)} %param.22) | copy-start | bytes 3145732
  16.0 0.8 copy-start.5
  16.8 1.5 copy-start.11
  16.8 1.5 copy-start.16
  18.3 3.7 %copy-start.1 = (bf16[1,256,4096]{2,1,0:T(8,128)(2,1)S(1)}, bf16[1,256,4096]{2,1,0:T(8,128)(2,1)}, u32[]{:S(2)}) copy-start(bf16[1,256,4096]{2,1,0:T(8,128)(2,1)} %param.19) | copy-start | bytes 6291460
  22.0 0.6 copy-start.10
  22.0 0.7 copy-start.15
  22.0 0.7 copy-start.9
  22.0 0.7 copy-start.13
  22.7 1.8 copy-start.6
  22.7 1.8 copy-start.8
  22.7 2.2 %copy-start.2 = (bf16[1,256,4096]{2,1,0:T(8,128)(2,1)S(1)}, bf16[1,256,4096]{2,1,0:T(8,128)(2,1)}, u32[]{:S(2)}) copy-start(bf16[1,256,4096]{2,1,0:T(8,128)(2,1)} %param.20) | copy-start | bytes 6291460
  25.4 1.2 copy-start.4
  25.4 1.2 copy-start.17
  25.4 2.8 %copy-start.14 = (bf16[512]{0:T(512)(128)(2,1)S(1)}, bf16[512]{0:T(512)(128)(2,1)}, u32[]{:S(2)}) copy-start(bf16[512]{0:T(512)(128)(2,1)} %param.27) | copy-start | bytes 3076
  25.4 2.8 %copy-start.7 = (bf16[4,4,512]{2,1,0:T(4,128)(2,1)S(1)}, bf16[4,4,512]{2,1,0:T(4,128)(2,1)}, u32[]{:S(2)}) copy-start(bf16[4,4,512]{2,1,0:T(4,128)(2,1)} %param.25) | copy-start | bytes 49156
  28.1 146.6 %all-gather.6.cloned.1.call-start = ((), (), s32[]{:S(2)}) async-start(), calls=%async_computation.3 | async-start | bytes 9437184 | tf_op jit(solution)/shard_map/all_gather | solution.py:152
  60.7 1.6 slice-start
  95.3 110.7 %reduce-scatter.2.cloned.1.call-start = ((), (), s32[]{:S(2)}) async-start(), calls=%async_computation.2 | async-start | bytes 163840 | tf_op jit(solution)/shard_map/reduce_scatter | solution.py:154
Sparse Core Ops, SparseCore 0:
  28.3 32.3 all-gather.3
  95.4 79.2 all-gather.5
  183.6 22.3 reduce-scatter.1
